TPU v7x, 32 devices: a whole 2x2x4 slice. The times are simulated.
32 devices in a mesh: depth: 4 (over x, core), lat: 8 (over z, y).
Axes of the slice: x: 2, y: 2, z: 4, core: 2. Of those that a mesh axis runs over, the one named last changes fastest.
Arguments:
- source: float32 [4, 2, 320, 32, 512], P(None, None, 'depth', 'lat'), may hold values from -6 to 6
- line_inverse: float32 [4, 2, 80, 80], P('depth'), may hold values from -0.6 to 1.6, as said below
- plane_count: int32 [4], P('depth'), may hold values from 48 to 80
- classes: int32 [320, 32, 512], P('depth', 'lat'), may hold values from 0 to 15
- table_re: float32 [16], replicated, may hold values from -2 to 2
- table_im: float32 [16], replicated, may hold values from 0.5 to 2
Outputs:
- field: float32 [4, 2, 320, 32, 512], P(None, None, 'depth', 'lat')
Inputs may be any that keep to these rules, and one draw needn't show every extreme that they name: `line_inverse`: a dense complex matrix for each layer whose real diagonal is about 0.8.
All inputs are finite; a program needn't handle non-finite values.
Results may differ from a plain program's by a relative error of at most 0.0001.
Values sent between devices are 32-bit elements; how exact they have to be, the bound alone decides.
No kernel may reach another device: no remote copies, remote signals or barrier semaphores. Data moves between devices by JAX's collectives and lax.ppermute only.
A program may use at most 128 MiB of HBM per device.

v0:
```python
import jax
import jax.numpy as jnp
from jax import lax
from jax.experimental import pallas as pl
from jax.experimental.pallas import tpu as pltpu
from jax.sharding import PartitionSpec as P

CORRECTION = 0.1
NEAR = CORRECTION * 4.0 / 3.0
FAR = -CORRECTION / 12.0
CENTER = 1.0 - 5.0 * CORRECTION
REACH = 2
PARAMS = pltpu.CompilerParams(vmem_limit_bytes=40 * 2**20)
COST = pl.CostEstimate(flops=0, bytes_accessed=0, transcendentals=0)


def call(kernel, **kwargs):
    return pl.pallas_call(kernel, compiler_params=PARAMS, cost_estimate=COST, **kwargs)


def whole(array):
    zeros = (0,) * array.ndim
    return pl.BlockSpec(array.shape, lambda *_: zeros)


SCALARS = pl.BlockSpec(memory_space=pltpu.SMEM)


def lookup(classes, re_ref, im_ref):
    kappa_re = jnp.zeros(classes.shape, jnp.float32)
    kappa_im = jnp.zeros(classes.shape, jnp.float32)
    for index in range(re_ref.shape[0]):
        hit = classes == index
        kappa_re = jnp.where(hit, re_ref[index], kappa_re)
        kappa_im = jnp.where(hit, im_ref[index], kappa_im)
    return kappa_re, kappa_im


def along_lanes(cells):
    axis = cells.ndim - 1
    width = cells.shape[axis]
    lane = lax.broadcasted_iota(jnp.int32, cells.shape, axis)
    right1 = jnp.where(lane >= 1, pltpu.roll(cells, 1, axis), 0.0)
    right2 = jnp.where(lane >= 2, pltpu.roll(cells, 2, axis), 0.0)
    left1 = jnp.where(lane < width - 1, pltpu.roll(cells, width - 1, axis), 0.0)
    left2 = jnp.where(lane < width - 2, pltpu.roll(cells, width - 2, axis), 0.0)
    return NEAR * (right1 + left1) + FAR * (right2 + left2)


def product(split_ref, cells):
    high = cells.astype(jnp.bfloat16)
    low = (cells - high.astype(jnp.float32)).astype(jnp.bfloat16)
    stacked = jnp.concatenate([high, high, low], axis=0)
    return jnp.dot(split_ref[...], stacked, preferred_element_type=jnp.float32)


def base_and_first(source, classes, matrix, count, parity, group):
    shots, _, planes, rows, width = source.shape
    half = shots // 2

    def kernel(count_ref, parity_ref, x_ref, last_ref, first_ref, matrix_ref, o_ref, near_ref):
        shot = pl.program_id(0)
        live = count_ref[0]
        row = lax.broadcasted_iota(jnp.int32, (planes, planes), 0)
        column = lax.broadcasted_iota(jnp.int32, (planes, planes), 1)
        wanted = jnp.where(shot < half, live - 1, 0)
        weights = []
        for c in range(2):
            picked = jnp.sum(jnp.where(row == wanted, matrix_ref[c], 0.0), axis=0, keepdims=True)
            spread = jnp.where((row == column) & (column < live), picked, 0.0)
            weights.append(jnp.sum(spread, axis=1, keepdims=True))
        a, b = weights

        @pl.when(shot == 0)
        def _():
            o_ref[2 * shots] = last_ref[0].astype(jnp.float32)
            o_ref[2 * shots + 1] = first_ref[0].astype(jnp.float32)

        for r in range(rows):
            re = x_ref[0, 0, :, r, :]
            im = x_ref[0, 1, :, r, :]
            o_ref[2 * shot, r:r + 1, :] = jnp.sum(a * re - b * im, axis=0, keepdims=True)
            o_ref[2 * shot + 1, r:r + 1, :] = jnp.sum(a * im + b * re, axis=0, keepdims=True)

        for odd in range(2):
            near_at = 0 if odd else rows - REACH

            @pl.when((parity_ref[0] == odd) & (shot < len(group)))
            def _():
                for j in range(REACH):
                    for c in range(2):
                        near_ref[0, j, c] = x_ref[0, c, :, near_at + j, :]

    near_out = (len(group), REACH, 2, planes, width)
    local_out = (2 * shots + 2, rows, width)
    return call(
        kernel,
        grid_spec=pltpu.PrefetchScalarGridSpec(
            num_scalar_prefetch=2,
            grid=(shots,),
            in_specs=[
                pl.BlockSpec((1, 2, planes, rows, width), lambda s, n, e: (s, 0, 0, 0, 0)),
                pl.BlockSpec((1, rows, width), lambda s, n, e: (n[0] - 1, 0, 0)),
                pl.BlockSpec((1, rows, width), lambda s, n, e: (0, 0, 0)),
                whole(matrix),
            ],
            out_specs=[
                pl.BlockSpec(local_out, lambda s, n, e: (0, 0, 0)),
                pl.BlockSpec(
                    (1,) + near_out[1:],
                    lambda s, n, e: (jnp.minimum(s, len(group) - 1), 0, 0, 0, 0),
                ),
            ],
        ),
        out_shape=[
            jax.ShapeDtypeStruct(local_out, jnp.float32),
            pltpu.HBM(near_out, jnp.float32),
        ],
        name="base_and_first",
    )(count, parity, source, classes, classes, matrix)


def pack(source, parity, near_groups, far_groups):
    shots, _, planes, rows, width = source.shape
    groups = near_groups + far_groups
    rows_out = (REACH, 2, planes, width)

    def kernel(parity_ref, x_ref, *refs):
        shot = pl.program_id(0)
        for odd in range(2):
            for k in range(shots):

                @pl.when((parity_ref[0] == odd) & (shot == k))
                def _():
                    for n, (ref, group) in enumerate(zip(refs, groups)):
                        if k not in group:
                            continue
                        at = 0 if (n < len(near_groups)) == bool(odd) else rows - REACH
                        for j in range(REACH):
                            for c in range(2):
                                ref[0, j, c] = x_ref[0, c, :, at + j, :]

    def spec(group):
        def at(s):
            return (jnp.clip(s - group[0], 0, len(group) - 1), 0, 0, 0, 0)

        return pl.BlockSpec((1,) + rows_out, at)

    outs = call(
        kernel,
        grid=(shots,),
        in_specs=[SCALARS, pl.BlockSpec((1, 2, planes, rows, width), lambda s: (s, 0, 0, 0, 0))],
        out_specs=[spec(group) for group in groups],
        out_shape=[pltpu.HBM((len(group),) + rows_out, jnp.float32) for group in groups],
        name="pack",
    )(parity, source)
    return outs[:len(near_groups)], outs[len(near_groups):]


def chain_start(tiles, table_re, table_im, matrix, count, place):
    entries, rows, width = tiles[0].shape
    shots = entries // 2 - 1
    planes = matrix.shape[-1]
    ext = -(-len(tiles) * rows // 8) * 8

    def kernel(re_ref, im_ref, count_ref, place_ref, matrix_ref, *refs):
        base_ref, kappa_ref, coeff_ref, inside_ref = refs[-4:]
        base_ref[...] = jnp.zeros_like(base_ref)
        kappa_ref[...] = jnp.zeros_like(kappa_ref)
        for j, ref in enumerate(refs[:-4]):
            span = pl.ds(j * rows, rows)
            for row in range(2 * shots):
                base_ref[row // 2, row % 2, span, :] = ref[row]
            for way in range(2):
                kappa_re, kappa_im = lookup(ref[2 * shots + way], re_ref, im_ref)
                kappa_ref[way, 0, span, :] = kappa_re
                kappa_ref[way, 1, span, :] = kappa_im
        row = lax.broadcasted_iota(jnp.int32, (planes, planes), 0)
        column = lax.broadcasted_iota(jnp.int32, (planes, planes), 1)
        last = count_ref[0] - 1
        for way, mask in enumerate(((row == last) & (column == 0), (row == 0) & (column == last))):
            for c in range(2):
                picked = jnp.sum(jnp.where(mask, matrix_ref[c], 0.0), axis=0, keepdims=True)
                picked = jnp.sum(picked, axis=1, keepdims=True)
                coeff_ref[way, c] = jnp.broadcast_to(picked, (1, width))
        at = place_ref[0] + lax.broadcasted_iota(jnp.int32, (ext, width), 0)
        inside_ref[...] = jnp.where((at >= 0) & (at < place_ref[1]), 1.0, 0.0)

    return call(
        kernel,
        in_specs=[SCALARS] * 4 + [whole(matrix)] + [whole(tile) for tile in tiles],
        out_shape=[
            jax.ShapeDtypeStruct((shots, 2, ext, width), jnp.float32),
            jax.ShapeDtypeStruct((2, 2, ext, width), jnp.float32),
            jax.ShapeDtypeStruct((2, 2, 1, width), jnp.float32),
            jax.ShapeDtypeStruct((ext, width), jnp.float32),
        ],
        name="chain_start",
    )(table_re, table_im, count, place, matrix, *tiles)


def chain_step(base, kappa, coeff, inside, way, arrived):
    shots, _, ext, width = base.shape
    half = shots // 2

    def kernel(way_ref, base_ref, kappa_ref, coeff_ref, inside_ref, *refs):
        o_ref = refs[-1]
        way = way_ref[0]
        k_re = CORRECTION * kappa_ref[way, 0]
        k_im = CORRECTION * kappa_ref[way, 1]
        for k in range(half):
            re = base_ref[way * half + k, 0]
            im = base_ref[way * half + k, 1]
            if arrived:
                t_re, t_im = refs[0][k, 0], refs[0][k, 1]
                c_re, c_im = coeff_ref[way, 0], coeff_ref[way, 1]
                re = re + (c_re * t_re - c_im * t_im)
                im = im + (c_re * t_im + c_im * t_re)
            for part, cells, mixed in (
                (0, re, k_re * re - k_im * im),
                (1, im, k_re * im + k_im * re),
            ):
                near = pltpu.roll(cells, 1, 0) + pltpu.roll(cells, ext - 1, 0)
                far = pltpu.roll(cells, 2, 0) + pltpu.roll(cells, ext - 2, 0)
                total = CENTER * cells + NEAR * near + FAR * far + along_lanes(cells) + mixed
                o_ref[k, part] = inside_ref[...] * total

    operands = (base, kappa, coeff, inside, *arrived)
    return call(
        kernel,
        in_specs=[SCALARS] + [whole(a) for a in operands],
        out_shape=jax.ShapeDtypeStruct((half, 2, ext, width), jnp.float32),
        name="chain_step",
    )(way, *operands)


def spot(planes, down, live):
    plane = lax.broadcasted_iota(jnp.int32, (planes, 1), 0)
    return jnp.where(plane == jnp.where(down, 0, live - 1), 1.0, 0.0)


def own_part(source, classes, table_re, table_im, split, trace, count):
    shots, _, planes, rows, width = source.shape
    half = shots // 2

    def kernel(re_ref, im_ref, count_ref, x_ref, class_ref, split_ref, t_ref, o_ref, v_ref, k_ref):
        @pl.when(pl.program_id(0) == 0)
        def _():
            for r in range(rows):
                kappa_re, kappa_im = lookup(class_ref[:, r, :], re_ref, im_ref)
                k_ref[r, 0] = CORRECTION * kappa_re
                k_ref[r, 1] = CORRECTION * kappa_im

        enters = spot(planes, pl.program_id(0) < half, count_ref[0])
        for r in range(rows):
            parts = [x_ref[0, c, :, r, :] + enters * t_ref[0, c, r:r + 1, :] for c in range(2)]
            v_ref[r] = product(split_ref, jnp.concatenate(parts, axis=0))
        for r in range(rows):
            fields = [v_ref[r, pl.ds(c * planes, planes), :] for c in range(2)]
            k_re, k_im = k_ref[r, 0], k_ref[r, 1]
            mixed = (
                k_re * fields[0] - k_im * fields[1],
                k_re * fields[1] + k_im * fields[0],
            )
            for c in range(2):
                total = CENTER * fields[c] + mixed[c] + along_lanes(fields[c])
                for by, weight in ((-2, FAR), (-1, NEAR), (1, NEAR), (2, FAR)):
                    if 0 <= r + by < rows:
                        total = total + weight * v_ref[r + by, pl.ds(c * planes, planes), :]
                o_ref[0, r, pl.ds(c * planes, planes), :] = total

    return call(
        kernel,
        grid=(shots,),
        in_specs=[
            SCALARS,
            SCALARS,
            SCALARS,
            pl.BlockSpec((1, 2, planes, rows, width), lambda s: (s, 0, 0, 0, 0)),
            whole(classes),
            whole(split),
            pl.BlockSpec((1,) + trace.shape[1:], lambda s: (s, 0, 0, 0)),
        ],
        out_specs=pl.BlockSpec((1, rows, 2 * planes, width), lambda s: (s, 0, 0, 0)),
        out_shape=jax.ShapeDtypeStruct((shots, rows, 2 * planes, width), jnp.float32),
        scratch_shapes=[
            pltpu.VMEM((rows, 2 * planes, width), jnp.float32),
            pltpu.VMEM((rows, 2, planes, width), jnp.float32),
        ],
        name="own_part",
    )(table_re, table_im, count, source, classes, split, trace)


def halo_part(field, inner, parity, count, shot, near, at, far, far_at, split, edge):
    shots, rows, _, width = inner.shape
    planes = near.shape[3]
    half = shots // 2
    blocks = 2 if width % 256 == 0 else 1
    part = width // blocks
    shape = (shots, 2, planes, rows, width)
    aliased = [] if field is None else [field]

    def kernel(parity_ref, count_ref, u_ref, split_ref, edge_ref, near_ref, far_ref, *refs):
        o_ref = refs[-1]
        even = parity_ref[0] == 0
        enters = spot(planes, shot < half, count_ref[0])

        def halo(j):
            parts = []
            for c in range(2):
                close = near_ref[0, j % REACH, c]
                distant = far_ref[0, j % REACH, c]
                there = jnp.where(even, distant, close) if j < REACH else jnp.where(even, close, distant)
                parts.append(there + enters * edge_ref[0, c, j:j + 1, :])
            return jnp.concatenate(parts, axis=0)

        before = [halo(j) for j in range(REACH)]
        after = [halo(REACH + j) for j in range(REACH)]
        edges = {
            0: NEAR * before[1] + FAR * before[0],
            1: FAR * before[1],
            rows - 2: FAR * after[0],
            rows - 1: NEAR * after[0] + FAR * after[1],
        }
        for r in range(rows):
            cells = u_ref[0, r]
            if r in edges:
                cells = cells + product(split_ref, edges[r])
            for c in range(2):
                o_ref[0, c, :, r, :] = cells[c * planes:(c + 1) * planes]

    def rows_spec(at):
        return pl.BlockSpec((1, REACH, 2, planes, part), lambda i: (at, 0, 0, 0, i))

    return call(
        kernel,
        grid=(blocks,),
        in_specs=[
            SCALARS,
            SCALARS,
            pl.BlockSpec((1, rows, 2 * planes, part), lambda i: (shot, 0, 0, i)),
            whole(split),
            pl.BlockSpec((1, 2, 2 * REACH, part), lambda i: (shot, 0, 0, i)),
            rows_spec(at),
            rows_spec(far_at),
        ]
        + [pl.BlockSpec(memory_space=pl.ANY) for _ in aliased],
        out_specs=pl.BlockSpec((1, 2, planes, rows, part), lambda i: (shot, 0, 0, 0, i)),
        out_shape=jax.ShapeDtypeStruct(shape, jnp.float32),
        input_output_aliases={7: 0} if aliased else {},
        name="halo_part",
    )(parity, count, inner, split, edge, near, far, *aliased)


def moved(rows, pairs):
    return lax.ppermute(rows, "lat", pairs)


def on_device(source, line_inverse, plane_count, classes, table_re, table_im):
    matrix = line_inverse[0]
    count = plane_count[0]
    source = pltpu.with_memory_space_constraint(source, pltpu.HBM)
    classes = pltpu.with_memory_space_constraint(classes, pltpu.HBM)
    shots, _, planes, rows, width = source.shape
    half = shots // 2
    tiles = lax.axis_size("lat")
    depths = lax.axis_size("depth")
    tile = lax.axis_index("lat")
    layer = lax.axis_index("depth")
    parity = jnp.reshape(tile % 2, (1,)).astype(jnp.int32)
    index = jnp.arange(planes, dtype=jnp.int32)
    live = (index < count).astype(jnp.float32)
    swap = [(i, i ^ 1) for i in range(tiles)]
    beyond = [(i, i + 1) for i in range(1, tiles - 1, 2)] + [(i + 1, i) for i in range(1, tiles - 1, 2)]

    near_groups = [list(range(half)), list(range(half, shots))]
    far_groups = [list(range(shots - 1)), [shots - 1]]
    local, near_first = base_and_first(
        source, classes, matrix, plane_count, parity, near_groups[0]
    )
    near, far = pack(source, parity, near_groups[1:], far_groups)
    local, near, far = lax.optimization_barrier((local, near, far))
    near = [moved(near_first, swap), *near]
    wide = -(-REACH * depths // rows)
    parts = []
    for by in range(-wide, wide + 1):
        if by == 0:
            parts.append(local)
        else:
            parts.append(moved(local, [(i, i - by) for i in range(tiles) if 0 <= i - by < tiles]))
    parts, near, far = lax.optimization_barrier((parts, near, far))
    near[1] = moved(near[1], swap)

    place = jnp.stack([(tile - wide) * rows, jnp.int32(tiles * rows)]).astype(jnp.int32)
    base_ext, kappa_ext, coeff, inside = chain_start(
        parts, table_re, table_im, matrix, plane_count, place
    )
    arrived = ()
    down = jnp.zeros((half, 2) + base_ext.shape[2:], jnp.float32)
    up = down
    for k in range(depths - 1):
        back = depths - 1 - k
        way = jnp.reshape(jnp.where(layer == k, 0, 1), (1,)).astype(jnp.int32)
        outbound = chain_step(base_ext, kappa_ext, coeff, inside, way, arrived)
        came = lax.ppermute(outbound, "depth", [(k, k + 1), (back, back - 1)])
        down = jnp.where(layer == k + 1, came, down)
        up = jnp.where(layer == back - 1, came, up)
        arrived = (came,)
    trace = jnp.concatenate([down, up], axis=0)
    start = wide * rows
    own = trace[:, :, start:start + rows]
    edge = jnp.concatenate(
        [trace[:, :, start - REACH:start], trace[:, :, start + rows:start + rows + REACH]], axis=2
    )

    masked = matrix * live[None, :, None] * live[None, None, :]
    full = jnp.concatenate(
        [
            jnp.concatenate([masked[0], -masked[1]], axis=1),
            jnp.concatenate([masked[1], masked[0]], axis=1),
        ],
        axis=0,
    )
    rounded = lax.reduce_precision(full, 8, 7)
    high = rounded.astype(jnp.bfloat16)
    split = jnp.concatenate([high, (full - rounded).astype(jnp.bfloat16), high], axis=1)
    inner = own_part(source, classes, table_re, table_im, split, own, plane_count)
    near, far, inner = lax.optimization_barrier((near, far, inner))
    far = [moved(rows_there, beyond) for rows_there in far]
    field = None
    for shot in range(shots):
        at, far_at = shot // half, shot // (shots - 1)
        field = halo_part(
            field,
            inner,
            parity,
            plane_count,
            shot,
            near[at],
            shot - near_groups[at][0],
            far[far_at],
            shot - far_groups[far_at][0],
            split,
            edge,
        )
    return field


def solution(mesh):
    in_specs = (
        P(None, None, "depth", "lat", None),
        P("depth", None, None, None),
        P("depth"),
        P("depth", "lat", None),
        P(),
        P(),
    )
    out_specs = P(None, None, "depth", "lat", None)
    return jax.shard_map(
        on_device, mesh=mesh, in_specs=in_specs, out_specs=out_specs, check_vma=False
    )
```

profile of v0, /device:TPU:24, one launch (start us, length us, event | category | flops | bytes accessed | tf_op | source)
XLA Modules:
  0.0 133.3 jit_solution(13138476115263630798)
XLA Ops:
  0.7 0.9 copy-done
  1.6 5.9 %base_and_first.1 = (f32[10,4,512]{2,1,0:T(4,128)S(1)}, f32[2,2,2,80,512]{4,3,2,1,0:T(8,128)}) custom-call(s32[1]{0:T(128)} %copy.13.count_ref, s32[1]{0:T(128)} %bitcast.parity_ref, f32[4,2,80,4,512]{4,3,2,1,0:T(4,128)} %x_ref.5, s32[80,4,512]{2,1,0:T(4,128)} %class_ref.1, s32[80,4,512]{2,1,0:T(4,128)} %class_ref.1, f32[2,80,80]{2,1,0:T(8,128)S(1)} %bitcast.15), custom_call_target="tpu_custom_call" | custom-call | tf_op jit(solution)/shard_map/base_and_first/pallas_call | solution.py:96
  7.4 1.5 %collective-permute-start.4 = (f32[2,2,2,80,512]{4,3,2,1,0:T(8,128)}, f32[2,2,2,80,512]{4,3,2,1,0:T(8,128)S(1)}, u32[]{:S(2)}, u32[]{:S(2)}) collective-permute-start(f32[2,2,2,80,512]{4,3,2,1,0:T(8,128)} %get-tuple-element.37), channel_id=1, source_target_pairs={{0,1},{1,0},{2,3},{3,2},{4,5},{5,4},{6,7},{7,6},{8,9},{9,8},{10,11... | collective-permute-start | bytes 3932168 | tf_op jit(solution)/shard_map/ppermute | solution.py:356
  8.9 5.3 %pack.1 = (f32[2,2,2,80,512]{4,3,2,1,0:T(8,128)}, f32[3,2,2,80,512]{4,3,2,1,0:T(8,128)}, f32[1,2,2,80,512]{4,3,2,1,0:T(8,128)}) custom-call(s32[1]{0:T(128)} %bitcast.parity_ref, f32[4,2,80,4,512]{4,3,2,1,0:T(4,128)} %x_ref.5), custom_call_target="tpu_custom_call" | custom-call | tf_op jit(solution)/shard_map/pack/pallas_call | solution.py:149
  14.3 2.3 %collective-permute-start.3 = (f32[10,4,512]{2,1,0:T(4,128)S(1)}, f32[10,4,512]{2,1,0:T(4,128)S(1)}, u32[]{:S(2)}, u32[]{:S(2)}) collective-permute-start(f32[10,4,512]{2,1,0:T(4,128)S(1)} %get-tuple-element.47.refs_2_), channel_id=1, source_target_pairs={{2,0},{3,1},{4,2},{5,3},{6,4},{7,5},{10,8},{11,9},{12,10},{13,11},... | collective-permute-start | bytes 245768 | tf_op jit(solution)/shard_map/ppermute | solution.py:356
  16.6 2.2 %collective-permute-start.2 = (f32[10,4,512]{2,1,0:T(4,128)S(1)}, f32[10,4,512]{2,1,0:T(4,128)S(1)}, u32[]{:S(2)}, u32[]{:S(2)}) collective-permute-start(f32[10,4,512]{2,1,0:T(4,128)S(1)} %get-tuple-element.47.refs_2_), channel_id=1, source_target_pairs={{1,0},{2,1},{3,2},{4,3},{5,4},{6,5},{7,6},{9,8},{10,9},{11,10},{12... | collective-permute-start | bytes 245768 | tf_op jit(solution)/shard_map/ppermute | solution.py:356
  18.8 3.6 %collective-permute-start.1 = (f32[10,4,512]{2,1,0:T(4,128)S(1)}, f32[10,4,512]{2,1,0:T(4,128)S(1)}, u32[]{:S(2)}, u32[]{:S(2)}) collective-permute-start(f32[10,4,512]{2,1,0:T(4,128)S(1)} %get-tuple-element.47.refs_2_), channel_id=1, source_target_pairs={{0,1},{1,2},{2,3},{3,4},{4,5},{5,6},{6,7},{8,9},{9,10},{10,11},{11... | collective-permute-start | bytes 245768 | tf_op jit(solution)/shard_map/ppermute | solution.py:356
  22.5 1.3 collective-permute-start
  23.8 17.9 %collective-permute-done.2.refs_3_ = f32[10,4,512]{2,1,0:T(4,128)S(1)} collective-permute-done((f32[10,4,512]{2,1,0:T(4,128)S(1)}, f32[10,4,512]{2,1,0:T(4,128)S(1)}, u32[]{:S(2)}, u32[]{:S(2)}) %collective-permute-start.2) | collective-permute-done | bytes 81952 | tf_op jit(solution)/shard_map/ppermute | solution.py:356
  41.7 0.1 pad_add_fusion.place_ref
  41.8 0.1 multiply_multiply_fusion
  41.9 0.8 chain_start.1
  42.7 0.3 chain_step.3
  43.0 1.3 collective-permute-start.6
  44.4 1.0 collective-permute-done.6.refs_0_
  45.4 0.3 chain_step.4
  45.7 0.7 collective-permute-start.7
  46.4 0.3 chain_step.5
  46.7 1.3 collective-permute-start.8
  48.0 0.1 fusion
  48.2 0.1 pad_maximum_fusion.split_ref
  48.3 8.1 %collective-permute-done.8 = f32[2,2,24,512]{3,2,1,0:T(8,128)S(1)} collective-permute-done((f32[2,2,24,512]{3,2,1,0:T(8,128)S(1)}, f32[2,2,24,512]{3,2,1,0:T(8,128)S(1)}, u32[]{:S(2)}, u32[]{:S(2)}) %collective-permute-start.8) | collective-permute-done | bytes 196640 | tf_op jit(solution)/shard_map/ppermute | solution.py:405
  56.5 13.1 %own_part.1.u_ref = f32[4,4,160,512]{3,2,1,0:T(8,128)S(1)} custom-call(f32[16]{0:T(128)S(1)} %copy-done.2, f32[16]{0:T(128)S(1)} %copy-done.3, s32[1]{0:T(128)} %copy.13.count_ref, f32[4,2,80,4,512]{4,3,2,1,0:T(4,128)} %x_ref.5, s32[80,4,512]{2,1,0:T(4,128)} %class_ref.1, bf16[160,480]{1,0:T(8,128)(2,1)S(1)} %pad_maximum_fusion.split_ref, ...), custom_call_target="tpu_custom_call" | custom-call | tf_op jit(solution)/shard_map/own_part/pallas_call | solution.py:272
  69.6 2.0 %collective-permute-done.5.near_ref = f32[2,2,2,80,512]{4,3,2,1,0:T(8,128)S(1)} collective-permute-done((f32[2,2,2,80,512]{4,3,2,1,0:T(8,128)}, f32[2,2,2,80,512]{4,3,2,1,0:T(8,128)S(1)}, u32[]{:S(2)}, u32[]{:S(2)}) %collective-permute-start.5) | collective-permute-done | bytes 1310752 | tf_op jit(solution)/shard_map/ppermute | solution.py:356
  71.6 3.2 %collective-permute-start.10 = (f32[3,2,2,80,512]{4,3,2,1,0:T(8,128)S(1)}, f32[3,2,2,80,512]{4,3,2,1,0:T(8,128)S(1)}, u32[]{:S(2)}, u32[]{:S(2)}) collective-permute-start(f32[3,2,2,80,512]{4,3,2,1,0:T(8,128)S(1)} %copy-done.4), channel_id=1, source_target_pairs={{1,2},{3,4},{5,6},{2,1},{4,3},{6,5},{9,10},{11,12},{13,14},{10,9},... | collective-permute-start | bytes 5898248 | tf_op jit(solution)/shard_map/ppermute | solution.py:356
  74.9 3.5 %collective-permute-start.9 = (f32[1,2,2,80,512]{4,3,2,1,0:T(8,128)S(1)}, f32[1,2,2,80,512]{4,3,2,1,0:T(8,128)S(1)}, u32[]{:S(2)}, u32[]{:S(2)}) collective-permute-start(f32[1,2,2,80,512]{4,3,2,1,0:T(8,128)S(1)} %copy-done.5), channel_id=1, source_target_pairs={{1,2},{3,4},{5,6},{2,1},{4,3},{6,5},{9,10},{11,12},{13,14},{10,9},... | collective-permute-start | bytes 1966088 | tf_op jit(solution)/shard_map/ppermute | solution.py:356
  78.4 41.8 %collective-permute-done.10.far_ref = f32[3,2,2,80,512]{4,3,2,1,0:T(8,128)S(1)} collective-permute-done((f32[3,2,2,80,512]{4,3,2,1,0:T(8,128)S(1)}, f32[3,2,2,80,512]{4,3,2,1,0:T(8,128)S(1)}, u32[]{:S(2)}, u32[]{:S(2)}) %collective-permute-start.10) | collective-permute-done | bytes 1966112 | tf_op jit(solution)/shard_map/ppermute | solution.py:356
  120.1 2.0 %halo_part.4.refs_0_ = f32[4,2,80,4,512]{4,3,2,1,0:T(4,128)} custom-call(s32[1]{0:T(128)} %bitcast.parity_ref, s32[1]{0:T(128)} %copy.13.count_ref, f32[4,4,160,512]{3,2,1,0:T(8,128)S(1)} %own_part.1.u_ref, bf16[160,480]{1,0:T(8,128)(2,1)S(1)} %pad_maximum_fusion.split_ref, f32[4,2,4,512]{3,2,1,0:T(4,128)S(1)} %get-tuple-element.61.edge_ref, ...), custom_call_target="tpu_custom_call" | custom-call | tf_op jit(solution)/shard_map/halo_part/pallas_call | solution.py:335
  122.1 2.0 %halo_part.5.refs_0_ = f32[4,2,80,4,512]{4,3,2,1,0:T(4,128)} custom-call(s32[1]{0:T(128)} %bitcast.parity_ref, s32[1]{0:T(128)} %copy.13.count_ref, f32[4,4,160,512]{3,2,1,0:T(8,128)S(1)} %own_part.1.u_ref, bf16[160,480]{1,0:T(8,128)(2,1)S(1)} %pad_maximum_fusion.split_ref, ...), custom_call_target="tpu_custom_call", output_to_operand_aliasing={{}: (7, {})} | custom-call | tf_op jit(solution)/shard_map/halo_part/pallas_call | solution.py:335
  124.1 2.0 %halo_part.6.refs_0_ = f32[4,2,80,4,512]{4,3,2,1,0:T(4,128)} custom-call(s32[1]{0:T(128)} %bitcast.parity_ref, s32[1]{0:T(128)} %copy.13.count_ref, f32[4,4,160,512]{3,2,1,0:T(8,128)S(1)} %own_part.1.u_ref, bf16[160,480]{1,0:T(8,128)(2,1)S(1)} %pad_maximum_fusion.split_ref, ...), custom_call_target="tpu_custom_call", output_to_operand_aliasing={{}: (7, {})} | custom-call | tf_op jit(solution)/shard_map/halo_part/pallas_call | solution.py:335
  126.1 5.2 %collective-permute-done.9.far_ref = f32[1,2,2,80,512]{4,3,2,1,0:T(8,128)S(1)} collective-permute-done((f32[1,2,2,80,512]{4,3,2,1,0:T(8,128)S(1)}, f32[1,2,2,80,512]{4,3,2,1,0:T(8,128)S(1)}, u32[]{:S(2)}, u32[]{:S(2)}) %collective-permute-start.9) | collective-permute-done | bytes 655392 | tf_op jit(solution)/shard_map/ppermute | solution.py:356
  131.3 2.0 %halo_part.7 = f32[4,2,80,4,512]{4,3,2,1,0:T(4,128)} custom-call(s32[1]{0:T(128)} %bitcast.parity_ref, s32[1]{0:T(128)} %copy.13.count_ref, f32[4,4,160,512]{3,2,1,0:T(8,128)S(1)} %own_part.1.u_ref, bf16[160,480]{1,0:T(8,128)(2,1)S(1)} %pad_maximum_fusion.split_ref, f32[4,2,4,512]{3,2,1,0:T(4,128)S(1)} %get-tuple-element.61.edge_ref, ...), custom_call_target="tpu_custom_call", output_to_operand_aliasing={{}: (7, {})} | custom-call | tf_op jit(solution)/shard_map/halo_part/pallas_call | solution.py:335
  (22 shorter events, 0.2 us)
Async XLA Ops:
  0.7 0.9 copy-start
  1.5 40.3 %copy-start.1 = (f32[1,2,80,80]{3,2,1,0:T(8,128)S(1)}, f32[1,2,80,80]{3,2,1,0:T(8,128)}, u32[]{:S(2)}) copy-start(f32[1,2,80,80]{3,2,1,0:T(8,128)} %param.7) | copy-start | bytes 153604
  1.5 40.4 %copy-start.2 = (f32[16]{0:T(128)S(1)}, f32[16]{0:T(128)}, u32[]{:S(2)}) copy-start(f32[16]{0:T(128)} %re_ref.3) | copy-start | bytes 196
  1.5 40.4 %copy-start.3 = (f32[16]{0:T(128)S(1)}, f32[16]{0:T(128)}, u32[]{:S(2)}) copy-start(f32[16]{0:T(128)} %im_ref.3) | copy-start | bytes 196
  7.4 34.2 %collective-permute-start.4 = (f32[2,2,2,80,512]{4,3,2,1,0:T(8,128)}, f32[2,2,2,80,512]{4,3,2,1,0:T(8,128)S(1)}, u32[]{:S(2)}, u32[]{:S(2)}) collective-permute-start(f32[2,2,2,80,512]{4,3,2,1,0:T(8,128)} %get-tuple-element.37), channel_id=1, source_target_pairs={{0,1},{1,0},{2,3},{3,2},{4,5},{5,4},{6,7},{7,6},{8,9},{9,8},{10,11... | collective-permute-start | bytes 3932168 | tf_op jit(solution)/shard_map/ppermute | solution.py:356
  14.3 9.5 %collective-permute-start.3 = (f32[10,4,512]{2,1,0:T(4,128)S(1)}, f32[10,4,512]{2,1,0:T(4,128)S(1)}, u32[]{:S(2)}, u32[]{:S(2)}) collective-permute-start(f32[10,4,512]{2,1,0:T(4,128)S(1)} %get-tuple-element.47.refs_2_), channel_id=1, source_target_pairs={{2,0},{3,1},{4,2},{5,3},{6,4},{7,5},{10,8},{11,9},{12,10},{13,11},... | collective-permute-start | bytes 245768 | tf_op jit(solution)/shard_map/ppermute | solution.py:356
  16.6 25.0 %collective-permute-start.2 = (f32[10,4,512]{2,1,0:T(4,128)S(1)}, f32[10,4,512]{2,1,0:T(4,128)S(1)}, u32[]{:S(2)}, u32[]{:S(2)}) collective-permute-start(f32[10,4,512]{2,1,0:T(4,128)S(1)} %get-tuple-element.47.refs_2_), channel_id=1, source_target_pairs={{1,0},{2,1},{3,2},{4,3},{5,4},{6,5},{7,6},{9,8},{10,9},{11,10},{12... | collective-permute-start | bytes 245768 | tf_op jit(solution)/shard_map/ppermute | solution.py:356
  18.8 22.8 %collective-permute-start.1 = (f32[10,4,512]{2,1,0:T(4,128)S(1)}, f32[10,4,512]{2,1,0:T(4,128)S(1)}, u32[]{:S(2)}, u32[]{:S(2)}) collective-permute-start(f32[10,4,512]{2,1,0:T(4,128)S(1)} %get-tuple-element.47.refs_2_), channel_id=1, source_target_pairs={{0,1},{1,2},{2,3},{3,4},{4,5},{5,6},{6,7},{8,9},{9,10},{10,11},{11... | collective-permute-start | bytes 245768 | tf_op jit(solution)/shard_map/ppermute | solution.py:356
  22.5 19.2 %collective-permute-start = (f32[10,4,512]{2,1,0:T(4,128)S(1)}, f32[10,4,512]{2,1,0:T(4,128)S(1)}, u32[]{:S(2)}, u32[]{:S(2)}) collective-permute-start(f32[10,4,512]{2,1,0:T(4,128)S(1)} %get-tuple-element.47.refs_2_), channel_id=1, source_target_pairs={{0,2},{1,3},{2,4},{3,5},{4,6},{5,7},{8,10},{9,11},{10,12},{11,13},... | collective-permute-start | bytes 245768 | tf_op jit(solution)/shard_map/ppermute | solution.py:356
  41.7 29.9 %collective-permute-start.5 = (f32[2,2,2,80,512]{4,3,2,1,0:T(8,128)}, f32[2,2,2,80,512]{4,3,2,1,0:T(8,128)S(1)}, u32[]{:S(2)}, u32[]{:S(2)}) collective-permute-start(f32[2,2,2,80,512]{4,3,2,1,0:T(8,128)} %get-tuple-element.42), channel_id=1, source_target_pairs={{0,1},{1,0},{2,3},{3,2},{4,5},{5,4},{6,7},{7,6},{8,9},{9,8},{10,11... | collective-permute-start | bytes 3932168 | tf_op jit(solution)/shard_map/ppermute | solution.py:356
  43.0 2.4 %collective-permute-start.6 = (f32[2,2,24,512]{3,2,1,0:T(8,128)S(1)}, f32[2,2,24,512]{3,2,1,0:T(8,128)S(1)}, u32[]{:S(2)}, u32[]{:S(2)}) collective-permute-start(f32[2,2,24,512]{3,2,1,0:T(8,128)S(1)} %chain_step.3), channel_id=1, source_target_pairs={{0,8},{24,16},{1,9},{25,17},{2,10},{26,18},{3,11},{27,19},{4,12},{... | collective-permute-start | bytes 589832 | tf_op jit(solution)/shard_map/ppermute | solution.py:405
  45.7 0.7 collective-permute-start.7
  46.7 9.6 %collective-permute-start.8 = (f32[2,2,24,512]{3,2,1,0:T(8,128)S(1)}, f32[2,2,24,512]{3,2,1,0:T(8,128)S(1)}, u32[]{:S(2)}, u32[]{:S(2)}) collective-permute-start(f32[2,2,24,512]{3,2,1,0:T(8,128)S(1)} %chain_step.5), channel_id=1, source_target_pairs={{16,24},{8,0},{17,25},{9,1},{18,26},{10,2},{19,27},{11,3},{20,28},... | collective-permute-start | bytes 589832 | tf_op jit(solution)/shard_map/ppermute | solution.py:405
  56.5 15.1 %copy-start.4 = (f32[3,2,2,80,512]{4,3,2,1,0:T(8,128)S(1)}, f32[3,2,2,80,512]{4,3,2,1,0:T(8,128)}, u32[]{:S(2)}) copy-start(f32[3,2,2,80,512]{4,3,2,1,0:T(8,128)} %get-tuple-element.57) | copy-start | bytes 5898244
  56.5 18.4 %copy-start.5 = (f32[1,2,2,80,512]{4,3,2,1,0:T(8,128)S(1)}, f32[1,2,2,80,512]{4,3,2,1,0:T(8,128)}, u32[]{:S(2)}) copy-start(f32[1,2,2,80,512]{4,3,2,1,0:T(8,128)} %get-tuple-element.56) | copy-start | bytes 1966084
  71.6 48.5 %collective-permute-start.10 = (f32[3,2,2,80,512]{4,3,2,1,0:T(8,128)S(1)}, f32[3,2,2,80,512]{4,3,2,1,0:T(8,128)S(1)}, u32[]{:S(2)}, u32[]{:S(2)}) collective-permute-start(f32[3,2,2,80,512]{4,3,2,1,0:T(8,128)S(1)} %copy-done.4), channel_id=1, source_target_pairs={{1,2},{3,4},{5,6},{2,1},{4,3},{6,5},{9,10},{11,12},{13,14},{10,9},... | collective-permute-start | bytes 5898248 | tf_op jit(solution)/shard_map/ppermute | solution.py:356
  74.9 56.4 %collective-permute-start.9 = (f32[1,2,2,80,512]{4,3,2,1,0:T(8,128)S(1)}, f32[1,2,2,80,512]{4,3,2,1,0:T(8,128)S(1)}, u32[]{:S(2)}, u32[]{:S(2)}) collective-permute-start(f32[1,2,2,80,512]{4,3,2,1,0:T(8,128)S(1)} %copy-done.5), channel_id=1, source_target_pairs={{1,2},{3,4},{5,6},{2,1},{4,3},{6,5},{9,10},{11,12},{13,14},{10,9},... | collective-permute-start | bytes 1966088 | tf_op jit(solution)/shard_map/ppermute | solution.py:356
where the time goes:
time: 135 us; the launch traced here: 133 us
  waiting for transfers between devices  75.9 us (56%)
  Pallas kernels  34 us (25%)
  starting transfers between devices  21.1 us (16%)
    ppermute x8, waiting for transfers between devices, moved(): return lax.ppermute(rows, 'lat', pairs)  66.8 us
    ppermute x8, starting transfers between devices, moved(): return lax.ppermute(rows, 'lat', pairs)  17.8 us
    pallas_call x1, Pallas kernels, own_part(): call(kernel, grid=(shots,), in_specs=[SCALARS, SCALARS, SCALARS, pl.Block...  13.1 us
    ppermute x3, waiting for transfers between devices, on_device(): came = lax.ppermute(outbound, 'depth', [(k, k + 1), (back, back - 1)])  9.12 us
    pallas_call x4, Pallas kernels, halo_part(): call(kernel, grid=(blocks,), in_specs=[SCALARS, SCALARS, pl.BlockSpec((1,...  8.01 us
    pallas_call x1, Pallas kernels, base_and_first(): call(kernel, grid_spec=pltpu.PrefetchScalarGridSpec(num_scalar_prefetch=2...  5.87 us
    pallas_call x1, Pallas kernels, pack(): call(kernel, grid=(shots,), in_specs=[SCALARS, pl.BlockSpec((1, 2, planes...  5.31 us
    ppermute x3, starting transfers between devices, on_device(): came = lax.ppermute(outbound, 'depth', [(k, k + 1), (back, back - 1)])  3.27 us
  transfers between devices with their start and end apart: 11, of which 6 were waited for; matrix products, arithmetic and copies ran while one was open for 0% of the time, Pallas kernels for 20%

commit v1 on v0

--- a/solution.py
+++ b/solution.py
@@ -54,11 +54,11 @@
     return jnp.dot(split_ref[...], stacked, preferred_element_type=jnp.float32)
 
 
-def base_and_first(source, classes, matrix, count, parity, group):
+def base_rows(source, classes, matrix, count):
     shots, _, planes, rows, width = source.shape
     half = shots // 2
 
-    def kernel(count_ref, parity_ref, x_ref, last_ref, first_ref, matrix_ref, o_ref, near_ref):
+    def kernel(count_ref, x_ref, last_ref, first_ref, matrix_ref, o_ref):
         shot = pl.program_id(0)
         live = count_ref[0]
         row = lax.broadcasted_iota(jnp.int32, (planes, planes), 0)
@@ -82,53 +82,35 @@
             o_ref[2 * shot, r:r + 1, :] = jnp.sum(a * re - b * im, axis=0, keepdims=True)
             o_ref[2 * shot + 1, r:r + 1, :] = jnp.sum(a * im + b * re, axis=0, keepdims=True)
 
-        for odd in range(2):
-            near_at = 0 if odd else rows - REACH
-
-            @pl.when((parity_ref[0] == odd) & (shot < len(group)))
-            def _():
-                for j in range(REACH):
-                    for c in range(2):
-                        near_ref[0, j, c] = x_ref[0, c, :, near_at + j, :]
-
-    near_out = (len(group), REACH, 2, planes, width)
     local_out = (2 * shots + 2, rows, width)
     return call(
         kernel,
         grid_spec=pltpu.PrefetchScalarGridSpec(
-            num_scalar_prefetch=2,
+            num_scalar_prefetch=1,
             grid=(shots,),
             in_specs=[
-                pl.BlockSpec((1, 2, planes, rows, width), lambda s, n, e: (s, 0, 0, 0, 0)),
-                pl.BlockSpec((1, rows, width), lambda s, n, e: (n[0] - 1, 0, 0)),
-                pl.BlockSpec((1, rows, width), lambda s, n, e: (0, 0, 0)),
+                pl.BlockSpec((1, 2, planes, rows, width), lambda s, n: (s, 0, 0, 0, 0)),
+                pl.BlockSpec((1, rows, width), lambda s, n: (n[0] - 1, 0, 0)),
+                pl.BlockSpec((1, rows, width), lambda s, n: (0, 0, 0)),
                 whole(matrix),
             ],
-            out_specs=[
-                pl.BlockSpec(local_out, lambda s, n, e: (0, 0, 0)),
-                pl.BlockSpec(
-                    (1,) + near_out[1:],
-                    lambda s, n, e: (jnp.minimum(s, len(group) - 1), 0, 0, 0, 0),
-                ),
-            ],
+            out_specs=pl.BlockSpec(local_out, lambda s, n: (0, 0, 0)),
         ),
-        out_shape=[
-            jax.ShapeDtypeStruct(local_out, jnp.float32),
-            pltpu.HBM(near_out, jnp.float32),
-        ],
-        name="base_and_first",
-    )(count, parity, source, classes, classes, matrix)
+        out_shape=jax.ShapeDtypeStruct(local_out, jnp.float32),
+        name="base_rows",
+    )(count, source, classes, classes, matrix)
 
 
 def pack(source, parity, near_groups, far_groups):
-    shots, _, planes, rows, width = source.shape
+    _, _, planes, rows, width = source.shape
     groups = near_groups + far_groups
+    chosen = sorted({shot for group in groups for shot in group})
     rows_out = (REACH, 2, planes, width)
 
     def kernel(parity_ref, x_ref, *refs):
-        shot = pl.program_id(0)
+        shot = pl.program_id(0) + chosen[0]
         for odd in range(2):
-            for k in range(shots):
+            for k in chosen:
 
                 @pl.when((parity_ref[0] == odd) & (shot == k))
                 def _():
@@ -142,14 +124,14 @@
 
     def spec(group):
         def at(s):
-            return (jnp.clip(s - group[0], 0, len(group) - 1), 0, 0, 0, 0)
+            return (jnp.clip(s + chosen[0] - group[0], 0, len(group) - 1), 0, 0, 0, 0)
 
         return pl.BlockSpec((1,) + rows_out, at)
 
     outs = call(
         kernel,
-        grid=(shots,),
-        in_specs=[SCALARS, pl.BlockSpec((1, 2, planes, rows, width), lambda s: (s, 0, 0, 0, 0))],
+        grid=(len(chosen),),
+        in_specs=[SCALARS, pl.BlockSpec((1, 2, planes, rows, width), lambda s: (s + chosen[0], 0, 0, 0, 0))],
         out_specs=[spec(group) for group in groups],
         out_shape=[pltpu.HBM((len(group),) + rows_out, jnp.float32) for group in groups],
         name="pack",
@@ -375,9 +357,9 @@
 
     near_groups = [list(range(half)), list(range(half, shots))]
     far_groups = [list(range(shots - 1)), [shots - 1]]
-    local, near_first = base_and_first(
-        source, classes, matrix, plane_count, parity, near_groups[0]
-    )
+    (near_first,), _ = pack(source, parity, near_groups[:1], [])
+    near_first, held = lax.optimization_barrier((near_first, matrix))
+    local = base_rows(source, classes, held, plane_count)
     near, far = pack(source, parity, near_groups[1:], far_groups)
     local, near, far = lax.optimization_barrier((local, near, far))
     near = [moved(near_first, swap), *near]
@@ -425,7 +407,6 @@
     high = rounded.astype(jnp.bfloat16)
     split = jnp.concatenate([high, (full - rounded).astype(jnp.bfloat16), high], axis=1)
     inner = own_part(source, classes, table_re, table_im, split, own, plane_count)
-    near, far, inner = lax.optimization_barrier((near, far, inner))
     far = [moved(rows_there, beyond) for rows_there in far]
     field = None
     for shot in range(shots):

time: 135 us -> 135 us (level)
  waiting for transfers between devices: 75.9 us -> 54.7 us
  local copies, waits for them, and re-layouts: 0.91 us -> 14.4 us
  Pallas kernels: 34 us -> 37.9 us
  other arithmetic: 0.49 us -> 3.42 us
    ppermute x8, waiting for transfers between devices: 66.8 us -> 49.6 us  [moved(): return lax.ppermute(rows, 'lat', pairs)]
    unnamed x12 -> x50, local copies, waits for them, and re-layouts: 0.9 us -> 14.4 us
    ppermute x3, waiting for transfers between devices: 9.12 us -> 5.1 us  [on_device(): came = lax.ppermute(outbound, 'depth', [(k, k + 1), (back, back - 1)])]
    pallas_call x3, Pallas kernels: 0.92 us -> 2.53 us  [chain_step(): call(kernel, in_specs=[SCALARS] + [whole(a) for a in operands], out_shape...]
    pallas_call x2 -> x3, Pallas kernels: 11.2 us -> 12.7 us  [the longest x2 8.03 us: pack(): call(kernel, grid=(len(chosen),), in_specs=[SCALARS, pl.BlockSpec((1, 2,...]
  transfers between devices with their start and end apart: 11 -> 11, of which waited for: 6 -> 4; matrix products, arithmetic and copies ran while one was open for 0% -> 3% of each run, Pallas kernels for 20% -> 24%
where the time goes in v1:
time: 135 us; the launch traced here: 133 us
  waiting for transfers between devices  54.7 us (41%)
  Pallas kernels  37.9 us (28%)
  starting transfers between devices  21.9 us (16%)
  local copies, waits for them, and re-layouts  14.4 us (11%)
  other arithmetic  3.42 us (3%)
    ppermute x8, waiting for transfers between devices, moved(): return lax.ppermute(rows, 'lat', pairs)  49.6 us
    ppermute x8, starting transfers between devices, moved(): return lax.ppermute(rows, 'lat', pairs)  17.8 us
    unnamed x50, local copies, waits for them, and re-layouts  14.4 us
    pallas_call x1, Pallas kernels, own_part(): call(kernel, grid=(shots,), in_specs=[SCALARS, SCALARS, SCALARS, pl.Block...  13 us
    pallas_call x4, Pallas kernels, halo_part(): call(kernel, grid=(blocks,), in_specs=[SCALARS, SCALARS, pl.BlockSpec((1,...  8.85 us
    pallas_call x2, Pallas kernels, pack(): call(kernel, grid=(len(chosen),), in_specs=[SCALARS, pl.BlockSpec((1, 2,...  8.03 us
    ppermute x3, waiting for transfers between devices, on_device(): came = lax.ppermute(outbound, 'depth', [(k, k + 1), (back, back - 1)])  5.1 us
    pallas_call x1, Pallas kernels, base_rows(): call(kernel, grid_spec=pltpu.PrefetchScalarGridSpec(num_scalar_prefetch=1...  4.72 us
  transfers between devices with their start and end apart: 11, of which 4 were waited for; matrix products, arithmetic and copies ran while one was open for 3% of the time, Pallas kernels for 24%

profile of v1, /device:TPU:24, one launch (start us, length us, event | category | flops | bytes accessed | tf_op | source)
XLA Modules:
  0.0 133.3 jit_solution(13720076573662924252)
XLA Ops:
  0.0 2.7 %pack.2 = f32[2,2,2,80,512]{4,3,2,1,0:T(8,128)} custom-call(s32[1]{0:T(128)} %bitcast.parity_ref, f32[4,2,80,4,512]{4,3,2,1,0:T(4,128)} %x_ref.7), custom_call_target="tpu_custom_call" | custom-call | tf_op jit(solution)/shard_map/pack/pallas_call | solution.py:131
  2.7 1.5 %collective-permute-start.4 = (f32[2,2,2,80,512]{4,3,2,1,0:T(8,128)}, f32[2,2,2,80,512]{4,3,2,1,0:T(8,128)S(1)}, u32[]{:S(2)}, u32[]{:S(2)}) collective-permute-start(f32[2,2,2,80,512]{4,3,2,1,0:T(8,128)} %pack.2), channel_id=1, source_target_pairs={{0,1},{1,0},{2,3},{3,2},{4,5},{5,4},{6,7},{7,6},{8,9},{9,8},{10,11... | collective-permute-start | bytes 3932168 | tf_op jit(solution)/shard_map/ppermute | solution.py:338
  4.2 5.3 %pack.3 = (f32[2,2,2,80,512]{4,3,2,1,0:T(8,128)}, f32[3,2,2,80,512]{4,3,2,1,0:T(8,128)}, f32[1,2,2,80,512]{4,3,2,1,0:T(8,128)}) custom-call(s32[1]{0:T(128)} %bitcast.parity_ref, f32[4,2,80,4,512]{4,3,2,1,0:T(4,128)} %x_ref.7), custom_call_target="tpu_custom_call" | custom-call | tf_op jit(solution)/shard_map/pack/pallas_call | solution.py:131
  10.2 4.7 %base_rows.1.refs_2_ = f32[10,4,512]{2,1,0:T(4,128)S(1)} custom-call(s32[1]{0:T(128)} %copy.13.count_ref, f32[4,2,80,4,512]{4,3,2,1,0:T(4,128)} %x_ref.7, s32[80,4,512]{2,1,0:T(4,128)} %class_ref.1, s32[80,4,512]{2,1,0:T(4,128)} %class_ref.1, f32[2,80,80]{2,1,0:T(8,128)S(1)} %bitcast.15), custom_call_target="tpu_custom_call" | custom-call | tf_op jit(solution)/shard_map/base_rows/pallas_call | solution.py:86
  14.9 2.4 %collective-permute-start.3 = (f32[10,4,512]{2,1,0:T(4,128)S(1)}, f32[10,4,512]{2,1,0:T(4,128)S(1)}, u32[]{:S(2)}, u32[]{:S(2)}) collective-permute-start(f32[10,4,512]{2,1,0:T(4,128)S(1)} %base_rows.1.refs_2_), channel_id=1, source_target_pairs={{2,0},{3,1},{4,2},{5,3},{6,4},{7,5},{10,8},{11,9},{12,10},{13,11},... | collective-permute-start | bytes 245768 | tf_op jit(solution)/shard_map/ppermute | solution.py:338
  17.3 2.2 %collective-permute-start.2 = (f32[10,4,512]{2,1,0:T(4,128)S(1)}, f32[10,4,512]{2,1,0:T(4,128)S(1)}, u32[]{:S(2)}, u32[]{:S(2)}) collective-permute-start(f32[10,4,512]{2,1,0:T(4,128)S(1)} %base_rows.1.refs_2_), channel_id=1, source_target_pairs={{1,0},{2,1},{3,2},{4,3},{5,4},{6,5},{7,6},{9,8},{10,9},{11,10},{12... | collective-permute-start | bytes 245768 | tf_op jit(solution)/shard_map/ppermute | solution.py:338
  19.5 3.6 %collective-permute-start.1 = (f32[10,4,512]{2,1,0:T(4,128)S(1)}, f32[10,4,512]{2,1,0:T(4,128)S(1)}, u32[]{:S(2)}, u32[]{:S(2)}) collective-permute-start(f32[10,4,512]{2,1,0:T(4,128)S(1)} %base_rows.1.refs_2_), channel_id=1, source_target_pairs={{0,1},{1,2},{2,3},{3,4},{4,5},{5,6},{6,7},{8,9},{9,10},{10,11},{11... | collective-permute-start | bytes 245768 | tf_op jit(solution)/shard_map/ppermute | solution.py:338
  23.1 1.3 collective-permute-start
  25.7 11.3 %collective-permute-done.2.refs_3_ = f32[10,4,512]{2,1,0:T(4,128)S(1)} collective-permute-done((f32[10,4,512]{2,1,0:T(4,128)S(1)}, f32[10,4,512]{2,1,0:T(4,128)S(1)}, u32[]{:S(2)}, u32[]{:S(2)}) %collective-permute-start.2) | collective-permute-done | bytes 81952 | tf_op jit(solution)/shard_map/ppermute | solution.py:338
  38.9 1.1 copy-done
  39.9 2.6 %collective-permute-start.10 = (f32[3,2,2,80,512]{4,3,2,1,0:T(8,128)}, f32[3,2,2,80,512]{4,3,2,1,0:T(8,128)S(1)}, u32[]{:S(2)}, u32[]{:S(2)}) collective-permute-start(f32[3,2,2,80,512]{4,3,2,1,0:T(8,128)} %get-tuple-element.47), channel_id=1, source_target_pairs={{1,2},{3,4},{5,6},{2,1},{4,3},{6,5},{9,10},{11,12},{13,14},{10,9},... | collective-permute-start | bytes 5898248 | tf_op jit(solution)/shard_map/ppermute | solution.py:338
  44.3 0.9 copy-done.11
  45.1 0.9 copy-done.13
  46.0 0.9 copy-done.15
  46.9 0.9 copy-done.17
  50.9 1.3 collective-permute-start.5
  52.2 4.1 %collective-permute-start.9 = (f32[1,2,2,80,512]{4,3,2,1,0:T(8,128)}, f32[1,2,2,80,512]{4,3,2,1,0:T(8,128)}, u32[]{:S(2)}, u32[]{:S(2)}) collective-permute-start(f32[1,2,2,80,512]{4,3,2,1,0:T(8,128)} %get-tuple-element.46), channel_id=1, source_target_pairs={{1,2},{3,4},{5,6},{2,1},{4,3},{6,5},{9,10},{11,12},{13,14},{10,9},... | collective-permute-start | bytes 1966088 | tf_op jit(solution)/shard_map/ppermute | solution.py:338
  56.3 1.0 chain_step.4
  57.3 1.3 collective-permute-start.6
  59.3 1.0 copy-done.3
  61.8 1.2 chain_step.5
  63.0 1.5 %collective-permute-start.7 = (f32[2,2,24,512]{3,2,1,0:T(8,128)S(1)}, f32[2,2,24,512]{3,2,1,0:T(8,128)S(1)}, u32[]{:S(2)}, u32[]{:S(2)}) collective-permute-start(f32[2,2,24,512]{3,2,1,0:T(8,128)S(1)} %chain_step.5), channel_id=1, source_target_pairs={{16,24},{8,0},{17,25},{9,1},{18,26},{10,2},{19,27},{11,3},{20,28},... | collective-permute-start | bytes 589832 | tf_op jit(solution)/shard_map/ppermute | solution.py:387
  64.5 0.9 fusion
  65.5 5.1 %collective-permute-done.7 = f32[2,2,24,512]{3,2,1,0:T(8,128)S(1)} collective-permute-done((f32[2,2,24,512]{3,2,1,0:T(8,128)S(1)}, f32[2,2,24,512]{3,2,1,0:T(8,128)S(1)}, u32[]{:S(2)}, u32[]{:S(2)}) %collective-permute-start.7) | collective-permute-done | bytes 196640 | tf_op jit(solution)/shard_map/ppermute | solution.py:387
  70.6 1.1 select_select_fusion.1
  73.0 13.0 %own_part.1.u_ref = f32[4,4,160,512]{3,2,1,0:T(8,128)S(1)} custom-call(f32[16]{0:T(128)S(1)} %copy-done.21, f32[16]{0:T(128)S(1)} %copy-done.23, s32[1]{0:T(128)} %copy.13.count_ref, f32[4,2,80,4,512]{4,3,2,1,0:T(4,128)} %x_ref.7, s32[80,4,512]{2,1,0:T(4,128)} %class_ref.1, bf16[160,480]{1,0:T(8,128)(2,1)S(1)} %pad_maximum_fusion.split_ref, ...), custom_call_target="tpu_custom_call" | custom-call | tf_op jit(solution)/shard_map/own_part/pallas_call | solution.py:254
  86.0 2.7 %collective-permute-done.10.far_ref = f32[3,2,2,80,512]{4,3,2,1,0:T(8,128)S(1)} collective-permute-done((f32[3,2,2,80,512]{4,3,2,1,0:T(8,128)}, f32[3,2,2,80,512]{4,3,2,1,0:T(8,128)S(1)}, u32[]{:S(2)}, u32[]{:S(2)}) %collective-permute-start.10) | collective-permute-done | bytes 1966112 | tf_op jit(solution)/shard_map/ppermute | solution.py:338
  88.7 2.0 %halo_part.4.refs_0_ = f32[4,2,80,4,512]{4,3,2,1,0:T(4,128)} custom-call(s32[1]{0:T(128)} %bitcast.parity_ref, s32[1]{0:T(128)} %copy.13.count_ref, f32[4,4,160,512]{3,2,1,0:T(8,128)S(1)} %own_part.1.u_ref, bf16[160,480]{1,0:T(8,128)(2,1)S(1)} %pad_maximum_fusion.split_ref, f32[4,2,4,512]{3,2,1,0:T(4,128)S(1)} %get-tuple-element.51.edge_ref, ...), custom_call_target="tpu_custom_call" | custom-call | tf_op jit(solution)/shard_map/halo_part/pallas_call | solution.py:317
  90.8 2.0 %halo_part.5.refs_0_ = f32[4,2,80,4,512]{4,3,2,1,0:T(4,128)} custom-call(s32[1]{0:T(128)} %bitcast.parity_ref, s32[1]{0:T(128)} %copy.13.count_ref, f32[4,4,160,512]{3,2,1,0:T(8,128)S(1)} %own_part.1.u_ref, bf16[160,480]{1,0:T(8,128)(2,1)S(1)} %pad_maximum_fusion.split_ref, ...), custom_call_target="tpu_custom_call", output_to_operand_aliasing={{}: (7, {})} | custom-call | tf_op jit(solution)/shard_map/halo_part/pallas_call | solution.py:317
  92.8 35.7 %collective-permute-done.8.near_ref = f32[2,2,2,80,512]{4,3,2,1,0:T(8,128)S(1)} collective-permute-done((f32[2,2,2,80,512]{4,3,2,1,0:T(8,128)}, f32[2,2,2,80,512]{4,3,2,1,0:T(8,128)S(1)}, u32[]{:S(2)}, u32[]{:S(2)}) %collective-permute-start.8) | collective-permute-done | bytes 1310752 | tf_op jit(solution)/shard_map/ppermute | solution.py:338
  128.4 2.0 %halo_part.6.refs_0_ = f32[4,2,80,4,512]{4,3,2,1,0:T(4,128)} custom-call(s32[1]{0:T(128)} %bitcast.parity_ref, s32[1]{0:T(128)} %copy.13.count_ref, f32[4,4,160,512]{3,2,1,0:T(8,128)S(1)} %own_part.1.u_ref, bf16[160,480]{1,0:T(8,128)(2,1)S(1)} %pad_maximum_fusion.split_ref, ...), custom_call_target="tpu_custom_call", output_to_operand_aliasing={{}: (7, {})} | custom-call | tf_op jit(solution)/shard_map/halo_part/pallas_call | solution.py:317
  130.4 2.8 %halo_part.7 = f32[4,2,80,4,512]{4,3,2,1,0:T(4,128)} custom-call(s32[1]{0:T(128)} %bitcast.parity_ref, s32[1]{0:T(128)} %copy.13.count_ref, f32[4,4,160,512]{3,2,1,0:T(8,128)S(1)} %own_part.1.u_ref, bf16[160,480]{1,0:T(8,128)(2,1)S(1)} %pad_maximum_fusion.split_ref, f32[4,2,4,512]{3,2,1,0:T(4,128)S(1)} %get-tuple-element.51.edge_ref, ...), custom_call_target="tpu_custom_call", output_to_operand_aliasing={{}: (7, {})} | custom-call | tf_op jit(solution)/shard_map/halo_part/pallas_call | solution.py:317
  (61 shorter events, 11.4 us)
Async XLA Ops:
  0.0 10.2 %copy-start.5 = (f32[1,2,80,80]{3,2,1,0:T(8,128)S(1)}, f32[1,2,80,80]{3,2,1,0:T(8,128)}, u32[]{:S(2)}) copy-start(f32[1,2,80,80]{3,2,1,0:T(8,128)} %param.7) | copy-start | bytes 153604
  2.7 36.1 %collective-permute-start.4 = (f32[2,2,2,80,512]{4,3,2,1,0:T(8,128)}, f32[2,2,2,80,512]{4,3,2,1,0:T(8,128)S(1)}, u32[]{:S(2)}, u32[]{:S(2)}) collective-permute-start(f32[2,2,2,80,512]{4,3,2,1,0:T(8,128)} %pack.2), channel_id=1, source_target_pairs={{0,1},{1,0},{2,3},{3,2},{4,5},{5,4},{6,7},{7,6},{8,9},{9,8},{10,11... | collective-permute-start | bytes 3932168 | tf_op jit(solution)/shard_map/ppermute | solution.py:338
  14.9 10.1 %collective-permute-start.3 = (f32[10,4,512]{2,1,0:T(4,128)S(1)}, f32[10,4,512]{2,1,0:T(4,128)S(1)}, u32[]{:S(2)}, u32[]{:S(2)}) collective-permute-start(f32[10,4,512]{2,1,0:T(4,128)S(1)} %base_rows.1.refs_2_), channel_id=1, source_target_pairs={{2,0},{3,1},{4,2},{5,3},{6,4},{7,5},{10,8},{11,9},{12,10},{13,11},... | collective-permute-start | bytes 245768 | tf_op jit(solution)/shard_map/ppermute | solution.py:338
  17.3 19.7 %collective-permute-start.2 = (f32[10,4,512]{2,1,0:T(4,128)S(1)}, f32[10,4,512]{2,1,0:T(4,128)S(1)}, u32[]{:S(2)}, u32[]{:S(2)}) collective-permute-start(f32[10,4,512]{2,1,0:T(4,128)S(1)} %base_rows.1.refs_2_), channel_id=1, source_target_pairs={{1,0},{2,1},{3,2},{4,3},{5,4},{6,5},{7,6},{9,8},{10,9},{11,10},{12... | collective-permute-start | bytes 245768 | tf_op jit(solution)/shard_map/ppermute | solution.py:338
  19.5 18.1 %collective-permute-start.1 = (f32[10,4,512]{2,1,0:T(4,128)S(1)}, f32[10,4,512]{2,1,0:T(4,128)S(1)}, u32[]{:S(2)}, u32[]{:S(2)}) collective-permute-start(f32[10,4,512]{2,1,0:T(4,128)S(1)} %base_rows.1.refs_2_), channel_id=1, source_target_pairs={{0,1},{1,2},{2,3},{3,4},{4,5},{5,6},{6,7},{8,9},{9,10},{10,11},{11... | collective-permute-start | bytes 245768 | tf_op jit(solution)/shard_map/ppermute | solution.py:338
  23.1 15.1 %collective-permute-start = (f32[10,4,512]{2,1,0:T(4,128)S(1)}, f32[10,4,512]{2,1,0:T(4,128)S(1)}, u32[]{:S(2)}, u32[]{:S(2)}) collective-permute-start(f32[10,4,512]{2,1,0:T(4,128)S(1)} %base_rows.1.refs_2_), channel_id=1, source_target_pairs={{0,2},{1,3},{2,4},{3,5},{4,6},{5,7},{8,10},{9,11},{10,12},{11,13},... | collective-permute-start | bytes 245768 | tf_op jit(solution)/shard_map/ppermute | solution.py:338
  37.0 0.6 copy-start.12
  37.6 0.6 copy-start.14
  38.9 1.1 copy-start
  39.9 48.8 %collective-permute-start.10 = (f32[3,2,2,80,512]{4,3,2,1,0:T(8,128)}, f32[3,2,2,80,512]{4,3,2,1,0:T(8,128)S(1)}, u32[]{:S(2)}, u32[]{:S(2)}) collective-permute-start(f32[3,2,2,80,512]{4,3,2,1,0:T(8,128)} %get-tuple-element.47), channel_id=1, source_target_pairs={{1,2},{3,4},{5,6},{2,1},{4,3},{6,5},{9,10},{11,12},{13,14},{10,9},... | collective-permute-start | bytes 5898248 | tf_op jit(solution)/shard_map/ppermute | solution.py:338
  42.6 85.8 %collective-permute-start.8 = (f32[2,2,2,80,512]{4,3,2,1,0:T(8,128)}, f32[2,2,2,80,512]{4,3,2,1,0:T(8,128)S(1)}, u32[]{:S(2)}, u32[]{:S(2)}) collective-permute-start(f32[2,2,2,80,512]{4,3,2,1,0:T(8,128)} %get-tuple-element.45), channel_id=1, source_target_pairs={{0,1},{1,0},{2,3},{3,2},{4,5},{5,4},{6,7},{7,6},{8,9},{9,8},{10,11... | collective-permute-start | bytes 3932168 | tf_op jit(solution)/shard_map/ppermute | solution.py:338
  43.4 0.9 copy-start.9
  44.3 0.9 copy-start.11
  45.1 0.9 copy-start.13
  46.0 0.9 copy-start.15
  46.9 0.9 copy-start.17
  47.8 0.7 copy-start.20
  48.5 0.7 copy-start.22
  50.5 5.8 %copy-start.2 = (f32[4,2,24,512]{3,2,1,0:T(8,128)}, f32[4,2,24,512]{3,2,1,0:T(8,128)S(1)}, u32[]{:S(2)}) copy-start(f32[4,2,24,512]{3,2,1,0:T(8,128)S(1)} %get-tuple-element.41.base_ref) | copy-start | bytes 1179652
  50.5 8.1 %copy-start.6 = (f32[24,512]{1,0:T(8,128)}, f32[24,512]{1,0:T(8,128)S(1)}, u32[]{:S(2)}) copy-start(f32[24,512]{1,0:T(8,128)S(1)} %get-tuple-element.44.inside_ref) | copy-start | bytes 147460
  50.5 8.1 %copy-start.18 = (f32[2,2,1,512]{3,2,1,0:T(1,128)}, f32[2,2,1,512]{3,2,1,0:T(1,128)S(1)}, u32[]{:S(2)}) copy-start(f32[2,2,1,512]{3,2,1,0:T(1,128)S(1)} %get-tuple-element.43.coeff_ref) | copy-start | bytes 24580
  50.9 5.4 %collective-permute-start.5 = (f32[2,2,24,512]{3,2,1,0:T(8,128)S(1)}, f32[2,2,24,512]{3,2,1,0:T(8,128)S(1)}, u32[]{:S(2)}, u32[]{:S(2)}) collective-permute-start(f32[2,2,24,512]{3,2,1,0:T(8,128)S(1)} %chain_step.3), channel_id=1, source_target_pairs={{0,8},{24,16},{1,9},{25,17},{2,10},{26,18},{3,11},{27,19},{4,12},{... | collective-permute-start | bytes 589832 | tf_op jit(solution)/shard_map/ppermute | solution.py:387
  52.2 78.2 %collective-permute-start.9 = (f32[1,2,2,80,512]{4,3,2,1,0:T(8,128)}, f32[1,2,2,80,512]{4,3,2,1,0:T(8,128)}, u32[]{:S(2)}, u32[]{:S(2)}) collective-permute-start(f32[1,2,2,80,512]{4,3,2,1,0:T(8,128)} %get-tuple-element.46), channel_id=1, source_target_pairs={{1,2},{3,4},{5,6},{2,1},{4,3},{6,5},{9,10},{11,12},{13,14},{10,9},... | collective-permute-start | bytes 1966088 | tf_op jit(solution)/shard_map/ppermute | solution.py:338
  56.3 1.0 copy-start.4
  57.3 2.0 %collective-permute-start.6 = (f32[2,2,24,512]{3,2,1,0:T(8,128)}, f32[2,2,24,512]{3,2,1,0:T(8,128)}, u32[]{:S(2)}, u32[]{:S(2)}) collective-permute-start(f32[2,2,24,512]{3,2,1,0:T(8,128)} %chain_step.4), channel_id=1, source_target_pairs={{8,16},{16,8},{9,17},{17,9},{10,18},{18,10},{11,19},{19,11},{12,20... | collective-permute-start | bytes 589832 | tf_op jit(solution)/shard_map/ppermute | solution.py:387
  59.3 1.0 copy-start.3
  60.3 0.8 copy-start.7
  61.1 0.7 copy-start.19
  63.0 7.6 %collective-permute-start.7 = (f32[2,2,24,512]{3,2,1,0:T(8,128)S(1)}, f32[2,2,24,512]{3,2,1,0:T(8,128)S(1)}, u32[]{:S(2)}, u32[]{:S(2)}) collective-permute-start(f32[2,2,24,512]{3,2,1,0:T(8,128)S(1)} %chain_step.5), channel_id=1, source_target_pairs={{16,24},{8,0},{17,25},{9,1},{18,26},{10,2},{19,27},{11,3},{20,28},... | collective-permute-start | bytes 589832 | tf_op jit(solution)/shard_map/ppermute | solution.py:387
  71.7 0.7 copy-start.21
  72.4 0.7 copy-start.23
  73.0 15.7 %copy-start.1 = (f32[2,2,2,80,512]{4,3,2,1,0:T(8,128)S(1)}, f32[2,2,2,80,512]{4,3,2,1,0:T(8,128)}, u32[]{:S(2)}) copy-start(f32[2,2,2,80,512]{4,3,2,1,0:T(8,128)} %copy-done) | copy-start | bytes 3932164
  (4 other events, 2.5 us)
